TPU v7x, 32 devices: a whole 2x2x4 slice. The times are simulated.
32 devices in a mesh: frame: 4 (over y, x), tile: 8 (over z, core).
Axes of the slice: x: 2, y: 2, z: 4, core: 2. Of those that a mesh axis runs over, the one named last changes fastest.
Arguments:
- point_feats: bfloat16 [4, 16, 81920], P('frame', None, 'tile'), may hold values from -6 to 6
- point_slot: int32 [4, 81920], P('frame', 'tile'), may hold values from 0 to 5119, as said below
- bucket_len: int32 [4, 64], P('frame', 'tile'), may hold values from 213 to 1280, as said below
- window_len: int32 [4, 320], P('frame', 'tile'), may hold values from 21 to 128, as said below
- w_vfe: bfloat16 [16, 128], replicated, may hold values from -1.5 to 1.5
- b_vfe: float32 [128], replicated, may hold values from -3 to 3
- gain_vfe: float32 [128], replicated, may hold values from 0.25 to 1.75
- w_qkv: bfloat16 [2, 128, 384], replicated, may hold values from -0.5 to 0.5
- b_qv: float32 [2, 256], replicated, may hold values from -2 to 2
- w_out: bfloat16 [2, 128, 128], replicated, may hold values from -1.5 to 1.5
- b_out: float32 [2, 128], replicated, may hold values from -2 to 2
- gain_attn: float32 [2, 128], replicated, may hold values from 0.25 to 1.75
- bias_attn: float32 [2, 128], replicated, may hold values from -2 to 2
- w_in: bfloat16 [2, 128, 256], replicated, may hold values from -0.5 to 0.5
- b_in: float32 [2, 256], replicated, may hold values from -3 to 3
- w_back: bfloat16 [2, 256, 128], replicated, may hold values from -0.375 to 0.375
- b_back: float32 [2, 128], replicated, may hold values from -2 to 2
- gain_ffn: float32 [2, 128], replicated, may hold values from 0.25 to 1.75
- bias_ffn: float32 [2, 128], replicated, may hold values from -2 to 2
- cotangent: bfloat16 [4, 40960, 128], P('frame', 'tile'), may hold values from -6 to 6
Outputs:
- pillar_out: bfloat16 [4, 40960, 128], P('frame', 'tile')
- grad_points: bfloat16 [4, 16, 81920], P('frame', None, 'tile')
- grad_w_vfe: float32 [16, 128], replicated
- grad_b_vfe: float32 [128], replicated
- grad_gain_vfe: float32 [128], replicated
- grad_w_qkv: float32 [2, 128, 384], replicated
- grad_b_qv: float32 [2, 256], replicated
- grad_w_out: float32 [2, 128, 128], replicated
- grad_b_out: float32 [2, 128], replicated
- grad_gain_attn: float32 [2, 128], replicated
- grad_bias_attn: float32 [2, 128], replicated
- grad_w_in: float32 [2, 128, 256], replicated
- grad_b_in: float32 [2, 256], replicated
- grad_w_back: float32 [2, 256, 128], replicated
- grad_b_back: float32 [2, 128], replicated
- grad_gain_ffn: float32 [2, 128], replicated
- grad_bias_ffn: float32 [2, 128], replicated
Inputs may be any that keep to these rules, and one draw needn't show every extreme that they name: `point_slot`: every point names a slot of an occupied pillar of its owner tile: its position in its window is below that window's length. `bucket_len`: live points of a bucket fill its first slots; in every frame every source fills its bucket for the last tile. `window_len`: occupied pillars of a window fill its first slots; the last tile's last window is full.
All inputs are finite; a program needn't handle non-finite values.
Results may differ from a plain program's by a relative error of at most 0.019.
Values may be sent and summed in bfloat16 or wider, within the bound.
A program may use at most 192 MiB of HBM per device.

v0:
```python
import jax
import jax.numpy as jnp
from jax import lax
from jax.sharding import PartitionSpec as P

HEADS = 8
WSLOT = 128
ATT_WIN = 4


NEG_FILL = -1e30
NORM_EPS = 1e-05


def passed_along(value, axis, steps):
    count = lax.axis_size(axis)
    pairs = [(source, (source + steps) % count) for source in range(count)]
    return lax.ppermute(value, axis, pairs)


def as_sent(x):
    return jax.tree.map(lambda a: a.astype(jnp.bfloat16) if a.dtype == jnp.float32 else a, x)


def gelu_tanh(values):
    return jax.nn.gelu(values, approximate=True)


def layer_norm(values, norm_gain, norm_bias):
    center = values - jnp.mean(values, axis=-1, keepdims=True)
    spread = jnp.mean(center * center, axis=-1, keepdims=True)
    return center * lax.rsqrt(spread + NORM_EPS) * norm_gain + norm_bias


def plain_product(left_side, right_side):
    return jnp.dot(left_side, right_side, preferred_element_type=jnp.float32)


def rows_product(left_side, right_side):
    return lax.dot_general(
        left_side, right_side, (((0,), (0,)), ((), ())), preferred_element_type=jnp.float32
    )


def by_transposed(left_side, right_side):
    return lax.dot_general(
        left_side, right_side, (((1,), (1,)), ((), ())), preferred_element_type=jnp.float32
    )


def split_blocks(values):
    row_count, model_width = values.shape
    return values.reshape(
        row_count // (ATT_WIN * WSLOT), ATT_WIN, WSLOT, HEADS, model_width // HEADS
    )


def block_scores(query_blk, key_blk, live_blk):
    scale_factor = query_blk.shape[-1] ** (-0.5)
    scores = (
        jnp.einsum("wqhd,wkhd->whqk", query_blk, key_blk, preferred_element_type=jnp.float32)
        * scale_factor
    )
    return jnp.where(live_blk[:, None, None, :] > 0.5, scores, NEG_FILL)


def attend_forward(queries, key_rows, val_rows, live_rows):

    def one_block(block_inputs):
        query_blk, key_blk, val_blk, live_blk = block_inputs
        masked = block_scores(query_blk, key_blk, live_blk)
        row_peak = jnp.max(masked, axis=-1, keepdims=True)
        denom_sum = jnp.sum(jnp.exp(masked - row_peak), axis=-1, keepdims=True)
        log_total = row_peak + jnp.log(denom_sum)
        weights_low = jnp.exp(masked - log_total).astype(jnp.bfloat16)
        mixture = jnp.einsum(
            "whqk,wkhd->wqhd", weights_low, val_blk, preferred_element_type=jnp.float32
        )
        return (mixture.astype(jnp.bfloat16), log_total)

    mixture, log_total = lax.map(
        one_block,
        (
            split_blocks(queries),
            split_blocks(key_rows),
            split_blocks(val_rows),
            live_rows.reshape(-1, ATT_WIN, WSLOT),
        ),
    )
    return (mixture.reshape(queries.shape), log_total)


def attend_backward(queries, key_rows, val_rows, live_rows, log_total, grad_mixture):

    def one_block(block_inputs):
        query_blk, key_blk, val_blk, live_blk, total_blk, grad_blk = block_inputs
        masked = block_scores(query_blk, key_blk, live_blk)
        weights_full = jnp.exp(masked - total_blk)
        weights_low = weights_full.astype(jnp.bfloat16)
        grad_val = jnp.einsum(
            "whqk,wqhd->wkhd", weights_low, grad_blk, preferred_element_type=jnp.float32
        )
        grad_weights = jnp.einsum(
            "wqhd,wkhd->whqk", grad_blk, val_blk, preferred_element_type=jnp.float32
        )
        row_dot = jnp.sum(weights_full * grad_weights, axis=-1, keepdims=True)
        grad_scores = (weights_full * (grad_weights - row_dot)).astype(jnp.bfloat16)
        scale_factor = query_blk.shape[-1] ** (-0.5)
        grad_query = (
            jnp.einsum("whqk,wkhd->wqhd", grad_scores, key_blk, preferred_element_type=jnp.float32)
            * scale_factor
        )
        grad_key = (
            jnp.einsum(
                "whqk,wqhd->wkhd", grad_scores, query_blk, preferred_element_type=jnp.float32
            )
            * scale_factor
        )
        return (
            grad_query.astype(jnp.bfloat16),
            grad_key.astype(jnp.bfloat16),
            grad_val.astype(jnp.bfloat16),
        )

    grad_query, grad_key, grad_val = lax.map(
        one_block,
        (
            split_blocks(queries),
            split_blocks(key_rows),
            split_blocks(val_rows),
            live_rows.reshape(-1, ATT_WIN, WSLOT),
            log_total,
            split_blocks(grad_mixture),
        ),
    )
    return (
        grad_query.reshape(queries.shape),
        grad_key.reshape(queries.shape),
        grad_val.reshape(queries.shape),
    )


def layer_forward(rows_in, live_rows, params):
    (
        w_qkv,
        b_qv,
        w_out,
        b_out,
        gain_attn,
        bias_attn,
        w_in,
        b_in,
        w_back,
        b_back,
        gain_ffn,
        bias_ffn,
    ) = params
    model_width = rows_in.shape[1]
    packed = plain_product(rows_in.astype(jnp.bfloat16), w_qkv)
    queries = (packed[:, :model_width] + b_qv[:model_width]).astype(jnp.bfloat16)
    key_rows = packed[:, model_width : 2 * model_width].astype(jnp.bfloat16)
    val_rows = (packed[:, 2 * model_width :] + b_qv[model_width:]).astype(jnp.bfloat16)
    mixture, log_total = attend_forward(queries, key_rows, val_rows, live_rows)
    first_sum = rows_in + (plain_product(mixture, w_out) + b_out)
    normed = layer_norm(first_sum, gain_attn, bias_attn)
    inner_pre = plain_product(normed.astype(jnp.bfloat16), w_in) + b_in
    inner_act = gelu_tanh(inner_pre).astype(jnp.bfloat16)
    second_sum = normed + (plain_product(inner_act, w_back) + b_back)
    result = layer_norm(second_sum, gain_ffn, bias_ffn) * live_rows[:, None]
    kept = (
        queries,
        key_rows,
        val_rows,
        mixture,
        log_total,
        first_sum,
        normed,
        inner_pre,
        inner_act,
        second_sum,
    )
    return (result, kept)


def layer_backward(grad_result, rows_in, live_rows, params, kept):
    (
        w_qkv,
        b_qv,
        w_out,
        b_out,
        gain_attn,
        bias_attn,
        w_in,
        b_in,
        w_back,
        b_back,
        gain_ffn,
        bias_ffn,
    ) = params
    (
        queries,
        key_rows,
        val_rows,
        mixture,
        log_total,
        first_sum,
        normed,
        inner_pre,
        inner_act,
        second_sum,
    ) = kept
    grad_masked = grad_result * live_rows[:, None]
    second_pull = jax.vjp(layer_norm, second_sum, gain_ffn, bias_ffn)[1]
    grad_second, grad_gain_ffn, grad_bias_ffn = second_pull(grad_masked)
    grad_outer = grad_second.astype(jnp.bfloat16)
    grad_w_back = rows_product(inner_act, grad_outer)
    grad_b_back = jnp.sum(grad_outer, axis=0, dtype=jnp.float32)
    grad_act = by_transposed(grad_outer, w_back)
    gelu_pull = jax.vjp(gelu_tanh, inner_pre)[1]
    grad_inner = gelu_pull(grad_act)[0].astype(jnp.bfloat16)
    grad_w_in = rows_product(normed.astype(jnp.bfloat16), grad_inner)
    grad_b_in = jnp.sum(grad_inner, axis=0, dtype=jnp.float32)
    grad_normed = grad_second + by_transposed(grad_inner, w_in)
    first_pull = jax.vjp(layer_norm, first_sum, gain_attn, bias_attn)[1]
    grad_first, grad_gain_attn, grad_bias_attn = first_pull(grad_normed)
    grad_branch = grad_first.astype(jnp.bfloat16)
    grad_w_out = rows_product(mixture, grad_branch)
    grad_b_out = jnp.sum(grad_branch, axis=0, dtype=jnp.float32)
    grad_mixture = by_transposed(grad_branch, w_out).astype(jnp.bfloat16)
    grad_query, grad_key, grad_val = attend_backward(
        queries, key_rows, val_rows, live_rows, log_total, grad_mixture
    )
    grad_packed = jnp.concatenate([grad_query, grad_key, grad_val], axis=1)
    grad_w_qkv = rows_product(rows_in.astype(jnp.bfloat16), grad_packed)
    grad_b_qv = jnp.concatenate(
        [
            jnp.sum(grad_query, axis=0, dtype=jnp.float32),
            jnp.sum(grad_val, axis=0, dtype=jnp.float32),
        ]
    )
    grad_rows = grad_first + by_transposed(grad_packed, w_qkv)
    grads = (
        grad_w_qkv,
        grad_b_qv,
        grad_w_out,
        grad_b_out,
        grad_gain_attn,
        grad_bias_attn,
        grad_w_in,
        grad_b_in,
        grad_w_back,
        grad_b_back,
        grad_gain_ffn,
        grad_bias_ffn,
    )
    return (grad_rows, grads)


def segment_rows(hidden_rows, targets, slot_count):
    return jax.ops.segment_sum(hidden_rows, targets, num_segments=slot_count + 1)[:slot_count]


def local(
    point_feats,
    point_slot,
    bucket_len,
    window_len,
    w_vfe,
    b_vfe,
    gain_vfe,
    w_qkv,
    b_qv,
    w_out,
    b_out,
    gain_attn,
    bias_attn,
    w_in,
    b_in,
    w_back,
    b_back,
    gain_ffn,
    bias_ffn,
    cotangent,
):
    tile_count = lax.axis_size("tile")
    feats_local = point_feats[0]
    feat_count, point_count = feats_local.shape
    bucket_size = point_count // tile_count
    slot_count = window_len.shape[1] * WSLOT
    point_live = (
        jnp.arange(bucket_size, dtype=jnp.int32)[None, :] < bucket_len[0][:, None]
    ).reshape(-1)
    live_float = point_live.astype(jnp.float32)
    slot_target = jnp.where(point_live, point_slot[0], slot_count)
    valid_rows = (
        (jnp.arange(WSLOT, dtype=jnp.int32)[None, :] < window_len[0][:, None])
        .reshape(-1)
        .astype(jnp.float32)
    )
    pre_act = rows_product(feats_local, w_vfe) + b_vfe
    hidden = gelu_tanh(pre_act) * live_float[:, None]
    got_hidden, got_slots = (
        lax.all_to_all(
            hidden.reshape(tile_count, bucket_size, -1),
            "tile",
            split_axis=0,
            concat_axis=0,
            tiled=True,
        ),
        lax.all_to_all(
            slot_target.astype(jnp.float32).reshape(tile_count, bucket_size),
            "tile",
            split_axis=0,
            concat_axis=0,
            tiled=True,
        ),
    )
    got_targets = got_slots.reshape(-1).astype(jnp.int32)
    pillar_sum = segment_rows(got_hidden.reshape(point_count, -1), got_targets, slot_count)
    squares, count_all = lax.psum(
        (jnp.sum(pillar_sum * pillar_sum * valid_rows[:, None], axis=0), jnp.sum(valid_rows)),
        "tile",
    )
    row_scale = lax.rsqrt(squares / count_all + NORM_EPS)
    encoded = pillar_sum * row_scale * gain_vfe
    stacked = (
        w_qkv,
        b_qv,
        w_out,
        b_out,
        gain_attn,
        bias_attn,
        w_in,
        b_in,
        w_back,
        b_back,
        gain_ffn,
        bias_ffn,
    )
    layer_zero = tuple((weight[0] for weight in stacked))
    layer_one = tuple((weight[1] for weight in stacked))
    half_slots = WSLOT // 2
    first_out, kept_zero = layer_forward(encoded, valid_rows, layer_zero)
    rim_values, rim_live = (
        passed_along(first_out[:half_slots].astype(jnp.bfloat16), "tile", -1).astype(jnp.float32),
        passed_along(valid_rows[:half_slots].astype(jnp.bfloat16), "tile", -1).astype(jnp.float32),
    )
    view_rows = jnp.concatenate([first_out[half_slots:], rim_values], axis=0)
    view_live = jnp.concatenate([valid_rows[half_slots:], rim_live], axis=0)
    view_out, kept_one = layer_forward(view_rows, view_live, layer_one)
    back_rim = passed_along(as_sent(view_out[-half_slots:]), "tile", 1)
    final_rows = jnp.concatenate([back_rim, view_out[:-half_slots]], axis=0)
    pillar_out = final_rows.astype(jnp.bfloat16)[None]
    cot_rows = cotangent[0]
    rim_cot = passed_along(cot_rows[:half_slots], "tile", -1)
    view_cot = jnp.concatenate([cot_rows[half_slots:], rim_cot], axis=0).astype(jnp.float32)
    grad_view, grads_one = layer_backward(view_cot, view_rows, view_live, layer_one, kept_one)
    back_grad = passed_along(as_sent(grad_view[-half_slots:]), "tile", 1)
    grad_first = jnp.concatenate([back_grad, grad_view[:-half_slots]], axis=0)
    grad_encoded, grads_zero = layer_backward(
        grad_first, encoded, valid_rows, layer_zero, kept_zero
    )
    local_dot = jnp.sum(grad_encoded * pillar_sum, axis=0)
    global_dot = lax.psum(local_dot, "tile")
    grad_gain_local = local_dot * row_scale
    grad_pillar = (
        grad_encoded * (gain_vfe * row_scale)
        - pillar_sum * valid_rows[:, None] * (gain_vfe * row_scale**3 * global_dot / count_all)
    ).astype(jnp.bfloat16)
    padded_grad = jnp.concatenate(
        [grad_pillar, jnp.zeros((1, grad_pillar.shape[1]), jnp.bfloat16)], axis=0
    )
    point_grad_rows = padded_grad[got_targets]
    grad_hidden = lax.all_to_all(
        point_grad_rows.reshape(tile_count, bucket_size, -1),
        "tile",
        split_axis=0,
        concat_axis=0,
        tiled=True,
    )
    gelu_pull = jax.vjp(gelu_tanh, pre_act)[1]
    grad_pre = gelu_pull(
        grad_hidden.reshape(point_count, -1).astype(jnp.float32) * live_float[:, None]
    )[0].astype(jnp.bfloat16)
    grad_w_vfe = plain_product(feats_local, grad_pre)
    grad_b_vfe = jnp.sum(grad_pre, axis=0, dtype=jnp.float32)
    grad_feats = by_transposed(w_vfe, grad_pre).astype(jnp.bfloat16)
    summed = lax.psum(
        (
            grad_w_vfe,
            grad_b_vfe,
            grad_gain_local,
            grads_zero[0],
            grads_zero[1],
            grads_zero[2],
            grads_zero[3],
            grads_zero[4],
            grads_zero[5],
            grads_zero[6],
            grads_zero[7],
            grads_zero[8],
            grads_zero[9],
            grads_zero[10],
            grads_zero[11],
            grads_one[0],
            grads_one[1],
            grads_one[2],
            grads_one[3],
            grads_one[4],
            grads_one[5],
            grads_one[6],
            grads_one[7],
            grads_one[8],
            grads_one[9],
            grads_one[10],
            grads_one[11],
        ),
        ("frame", "tile"),
    )
    vfe_sums = summed[:3]
    sums_zero = summed[3:15]
    sums_one = summed[15:]
    layer_grads = [
        jnp.stack([lower_grad, upper_grad]) for lower_grad, upper_grad in zip(sums_zero, sums_one)
    ]
    return (
        pillar_out,
        grad_feats[None],
        vfe_sums[0],
        vfe_sums[1],
        vfe_sums[2],
        layer_grads[0],
        layer_grads[1],
        layer_grads[2],
        layer_grads[3],
        layer_grads[4],
        layer_grads[5],
        layer_grads[6],
        layer_grads[7],
        layer_grads[8],
        layer_grads[9],
        layer_grads[10],
        layer_grads[11],
    )


def solution(mesh):
    placed = (
        P("frame", None, "tile"),
        P("frame", "tile"),
        P("frame", "tile"),
        P("frame", "tile"),
        P(),
        P(),
        P(),
        P(),
        P(),
        P(),
        P(),
        P(),
        P(),
        P(),
        P(),
        P(),
        P(),
        P(),
        P(),
        P("frame", "tile", None),
    )
    return jax.shard_map(
        local,
        mesh=mesh,
        in_specs=placed,
        out_specs=(
            P("frame", "tile", None),
            P("frame", None, "tile"),
            P(),
            P(),
            P(),
            P(),
            P(),
            P(),
            P(),
            P(),
            P(),
            P(),
            P(),
            P(),
            P(),
            P(),
            P(),
        ),
        check_vma=False,
    )
```

profile of v0, /device:TPU:0, one launch (start us, length us, event | category | flops | bytes accessed | tf_op | source)
XLA Modules:
  0.0 1078.3 jit_solution(6177230159060536515)
XLA Ops:
  8.8 6.3 all-to-all-start
  15.8 7.3 multiply_multiply_fusion.6
  23.2 5.2 all-to-all-start.1
  39.7 74.3 %collective-permute-done.1 = bf16[64]{0:T(256)(128)(2,1)S(1)} collective-permute-done((bf16[64]{0:T(256)(128)(2,1)S(1)}, bf16[64]{0:T(256)(128)(2,1)S(1)}, u32[]{:S(2)}, u32[]{:S(2)}) %collective-permute-start.1) | collective-permute-done | bytes 160 | tf_op jit(solution)/shard_map/ppermute | solution.py:18
  114.8 30.3 %all-to-all-done.1 = f32[8,1280,128]{2,1,0:T(8,128)} async-done(((f32[8,1280,128]{2,1,0:T(8,128)}), f32[8,1280,128]{2,1,0:T(8,128)}, u32[]{:S(2)}, u32[]{:S(2)}) %all-to-all-start.1) | async-done | bytes 5242912 | tf_op jit(solution)/shard_map/all_to_all | solution.py:303
  145.1 67.8 %scatter_custom_fusion = f32[5121,128]{1,0:T(8,128)S(1)} fusion(s32[10240]{0:T(1024)S(1)} %bitcast.437, f32[10240,128]{1,0:T(8,128)} %bitcast.43, f32[]{:T(128)} %constant.135.clone.1), kind=kCustom, calls=%fused_computation.225 | custom fusion | flops 1310720 | bytes 2622464 | tf_op jit(solution)/shard_map/scatter-add | solution.py:260
  215.1 14.4 %all-reduce.3 = (f32[128]{0:T(128)S(1)}, f32[]{:T(128)}) all-reduce(f32[128]{0:T(128)S(1)} %multiply_reduce_fusion.15, f32[]{:T(128)} %convert_reduce_fusion.11), channel_id=1, replica_groups=mesh['frame'=4,'tile'=8] {'tile'}, use_global_device_ids=true, to_apply=%region_2.3 | all-reduce | flops 129 | bytes 1032 | tf_op jit(solution)/shard_map/psum | solution.py:320
  237.5 3.7 reshape.498
  246.2 3.7 reshape.499
  255.0 3.7 reshape.497
  262.8 48.0 %while.52 = (s32[]{:T(128)}, bf16[10,4,128,8,16]{2,1,0,4,3:T(4,128)(2,1)}, f32[10,4,8,128,1]{3,2,1,4,0:T(8,128)S(1)}, bf16[10,4,128,8,16]{2,4,3,1,0:T(8,128)(2,1...) while((s32[]{:T(128)}, ...), condition=%wide.region_8.9_spmd, body=%wide.region_5.8_spmd.sunk | while | flops 37286400 | bytes 7213165 | solution.py:81
  341.8 3.7 reshape.503
  350.6 3.7 reshape.504
  359.4 3.7 reshape.501
  367.2 48.2 %while.53 = (s32[]{:T(128)}, bf16[10,4,128,8,16]{2,1,0,4,3:T(4,128)(2,1)}, f32[10,4,8,128,1]{3,2,1,4,0:T(8,128)S(1)}, bf16[10,4,128,8,16]{2,4,3,1,0:T(8,128)(2,1...) while((s32[]{:T(128)}, ...), condition=%wide.region_16.17_spmd, body=%wide.region_13.16_spmd.sunk | while | flops 37286400 | bytes 7213165 | solution.py:81
  435.1 3.8 multiply_reduce_fusion.2
  439.0 7.4 fusion.173
  451.9 4.3 convert_reduce_fusion
  480.1 111.3 %while.54 = (s32[]{:T(128)}, bf16[10,4,128,8,16]{2,4,3,1,0:T(8,128)(2,1)}, bf16[10,4,128,8,16]{2,1,0,4,3:T(4,128)(2,1)}, bf16[10,4,128,8,16]{2,4,3,1,0:T(8,128)(...) while((s32[]{:T(128)}, ...), condition=%wide.region_27.28_spmd, body=%wide.region_25.27_spmd.sunk | while | flops 88928768 | bytes 17650832 | solution.py:125
  614.7 4.2 convolution_add_fusion.4
  630.5 3.9 fusion.171
  636.7 4.1 convert_reduce_fusion.1
  656.7 105.1 %while.55 = (s32[]{:T(128)}, bf16[10,4,128,8,16]{2,4,3,1,0:T(8,128)(2,1)S(1)}, bf16[10,4,128,8,16]{2,1,0,4,3:T(4,128)(2,1)}, bf16[10,4,128,8,16]{2,4,3,1,0:T(8,1...) while((s32[]{:T(128)}, ...), condition=%wide.region_34.35_spmd, body=%wide.region_32.34_spmd.sunk | while | flops 88928768 | bytes 17650832 | solution.py:125
  761.8 3.8 reshape.512
  779.1 4.3 multiply_reduce_fusion.6
  783.3 14.1 %psum.212 = f32[128]{0:T(128)S(1)} all-reduce(f32[128]{0:T(128)S(1)} %get-tuple-element.525), channel_id=1, replica_groups=mesh['frame'=4,'tile'=8] {'tile'}, use_global_device_ids=true, to_apply=%region_36.37 | all-reduce | flops 128 | bytes 1024 | tf_op jit(solution)/shard_map/psum | solution.py:364
  802.4 36.4 %gather_fusion = bf16[10240,128]{1,0:T(8,128)(2,1)} fusion(bf16[5121,128]{1,0:T(8,128)(2,1)S(1)} %concatenate.51, s32[10240]{0:T(1024)S(1)} %copy-done.53), kind=kCustom, calls=%fused_computation | custom fusion | bytes 5283840 | tf_op jit(solution)/shard_map/gather | solution.py:373
  838.8 4.7 all-to-all-start.2
  856.0 5.2 convolution_bitcast_fusion.3
  862.4 149.1 %all-reduce.6.cloned.1.call-done = (f32[1,128,384]{2,1,0:T(8,128)}, f32[1,128,384]{2,1,0:T(8,128)}, f32[1,128,128]{2,1,0:T(8,128)}, f32[1,128,128]{2,1,0:T(8,128...) async-done(((f32[1,128,384]{2,1,0:T(8,128)}, f32[1,128,384]{2,1,0:T(8,128)}, f32[1,128,128]{2,1,0:T(8,128)}, ...) | async-done | bytes 1048592 | tf_op jit(solution)/shard_map/psum | solution.py:388
  1018.2 6.6 convert_reduce_fusion.2
  1027.1 39.5 %all-reduce.1 = (f32[16,128]{1,0:T(8,128)}, f32[128]{0:T(128)}, f32[128]{0:T(128)}, f32[1,256]{1,0:T(1,128)S(1)}, f32[1,256]{1,0:T(1,128)S(1)}, /*index=5*/f32[1...) all-reduce(f32[16,128]{1,0:T(8,128)S(1)} %convolution_bitcast_fusio, ...), channel_id=1, replica_groups=mesh['frame'=4,'tile'=8] {'frame','tile'}, use_global_device_ids=true, to_apply=%region_37.38 | all-reduce | flops 4864 | bytes 38912 | tf_op jit(solution)/shard_map/psum | solution.py:388
  (668 shorter events, 542.1 us)
Async XLA Ops:
  7.2 8.6 copy-start
  8.8 14.4 %all-to-all-start = ((f32[8,1,1280]{2,1,0:T(1,128)}), f32[8,1,1280]{2,1,0:T(1,128)S(1)}, u32[]{:S(2)}, u32[]{:S(2)}) async-start(f32[8,1,1280]{2,1,0:T(1,128)} %fusion.147), calls=%async_computation | async-start | bytes 81920 | tf_op jit(solution)/shard_map/all_to_all | solution.py:310
  15.8 7.3 copy-start.51
  23.1 9.1 copy-start.35
  23.1 12.0 %copy-start.75 = (f32[2,128]{1,0:T(2,128)S(1)}, f32[2,128]{1,0:T(2,128)}, u32[]{:S(2)}) copy-start(f32[2,128]{1,0:T(2,128)} %param.38) | copy-start | bytes 3076
  23.2 12.5 %copy-start.76 = (f32[2,128]{1,0:T(2,128)S(1)}, f32[2,128]{1,0:T(2,128)}, u32[]{:S(2)}) copy-start(f32[2,128]{1,0:T(2,128)} %param.39) | copy-start | bytes 3076
  23.2 13.0 %copy-start.72 = (f32[2,256]{1,0:T(2,128)S(1)}, f32[2,256]{1,0:T(2,128)}, u32[]{:S(2)}) copy-start(f32[2,256]{1,0:T(2,128)} %param.36) | copy-start | bytes 6148
  23.2 13.0 %copy-start.73 = (f32[2,256]{1,0:T(2,128)S(1)}, f32[2,256]{1,0:T(2,128)}, u32[]{:S(2)}) copy-start(f32[2,256]{1,0:T(2,128)} %param.42) | copy-start | bytes 6148
  23.2 13.6 %copy-start.77 = (f32[2,128]{1,0:T(2,128)S(1)}, f32[2,128]{1,0:T(2,128)}, u32[]{:S(2)}) copy-start(f32[2,128]{1,0:T(2,128)} %param.44) | copy-start | bytes 3076
  23.2 13.6 %copy-start.78 = (f32[2,128]{1,0:T(2,128)S(1)}, f32[2,128]{1,0:T(2,128)}, u32[]{:S(2)}) copy-start(f32[2,128]{1,0:T(2,128)} %param.40) | copy-start | bytes 3076
  23.2 14.1 %copy-start.79 = (f32[2,128]{1,0:T(2,128)S(1)}, f32[2,128]{1,0:T(2,128)}, u32[]{:S(2)}) copy-start(f32[2,128]{1,0:T(2,128)} %param.46) | copy-start | bytes 3076
  23.2 14.1 %copy-start.80 = (f32[2,128]{1,0:T(2,128)S(1)}, f32[2,128]{1,0:T(2,128)}, u32[]{:S(2)}) copy-start(f32[2,128]{1,0:T(2,128)} %param.45) | copy-start | bytes 3076
  23.2 121.8 %all-to-all-start.1 = ((f32[8,1280,128]{2,1,0:T(8,128)}), f32[8,1280,128]{2,1,0:T(8,128)}, u32[]{:S(2)}, u32[]{:S(2)}) async-start(f32[8,1280,128]{2,1,0:T(8,128)} %bitcast.431), calls=%async_computation.1 | async-start | bytes 10485760 | tf_op jit(solution)/shard_map/all_to_all | solution.py:303
  28.6 85.4 %collective-permute-start.1 = (bf16[64]{0:T(256)(128)(2,1)S(1)}, bf16[64]{0:T(256)(128)(2,1)S(1)}, u32[]{:S(2)}, u32[]{:S(2)}) collective-permute-start(bf16[64]{0:T(256)(128)(2,1)S(1)} %slice.325), channel_id=1, source_target_pairs={{0,7},{1,0},{2,1},{3,2},{4,3},{5,4},{6,5},{7,6},{8,15},{9,8},{10,9... | collective-permute-start | bytes 392 | tf_op jit(solution)/shard_map/ppermute | solution.py:18
  32.8 402.3 %collective-permute-start.3 = (bf16[64,128]{1,0:T(8,128)(2,1)}, bf16[64,128]{1,0:T(8,128)(2,1)S(1)}, u32[]{:S(2)}, u32[]{:S(2)}) collective-permute-start(bf16[64,128]{1,0:T(8,128)(2,1)} %slice_bitcast_fusion.2), channel_id=1, source_target_pairs={{0,7},{1,0},{2,1},{3,2},{4,3},{5,4},{6,5},{7,6},{8,15},{9,8},{10,9... | collective-permute-start | bytes 49160 | tf_op jit(solution)/shard_map/ppermute | solution.py:18
  36.2 287.8 %copy-start.59 = (f32[128]{0:T(128)}, f32[128]{0:T(128)S(1)}, u32[]{:S(2)}) copy-start(f32[128]{0:T(128)S(1)} %get-tuple-element.504) | copy-start | bytes 1540
  37.8 292.1 %copy-start.62 = (f32[128]{0:T(128)}, f32[128]{0:T(128)S(1)}, u32[]{:S(2)}) copy-start(f32[128]{0:T(128)S(1)} %get-tuple-element.533) | copy-start | bytes 1540
  145.1 84.4 %copy-start.54 = (f32[128]{0:T(128)S(1)}, f32[128]{0:T(128)}, u32[]{:S(2)}) copy-start(f32[128]{0:T(128)} %param.34) | copy-start | bytes 1540
  145.1 85.6 %copy-start.36 = (bf16[2,128,384]{2,1,0:T(8,128)(2,1)S(1)}, bf16[2,128,384]{2,1,0:T(8,128)(2,1)}, u32[]{:S(2)}) copy-start(bf16[2,128,384]{2,1,0:T(8,128)(2,1)} %param.35) | copy-start | bytes 589828
  212.9 101.5 %copy-start.1 = (f32[5121,128]{1,0:T(8,128)}, f32[5121,128]{1,0:T(8,128)S(1)}, u32[]{:S(2)}) copy-start(f32[5121,128]{1,0:T(8,128)S(1)} %scatter_custom_fusion) | copy-start | bytes 7865860
  230.7 83.7 %copy-start.56 = (f32[128]{0:T(128)}, f32[128]{0:T(128)S(1)}, u32[]{:S(2)}) copy-start(f32[128]{0:T(128)S(1)} %get-tuple-element.471) | copy-start | bytes 1540
  316.8 7.2 copy-start.4
  333.2 1.5 collective-permute-start
  619.6 241.7 %collective-permute-start.2 = (bf16[64,128]{1,0:T(8,128)(2,1)S(1)}, bf16[64,128]{1,0:T(8,128)(2,1)S(1)}, u32[]{:S(2)}, u32[]{:S(2)}) collective-permute-start(bf16[64,128]{1,0:T(8,128)(2,1)S(1)} %slice.210), channel_id=1, source_target_pairs={{0,1},{1,2},{2,3},{3,4},{4,5},{5,6},{6,7},{7,0},{8,9},{9,10},{10,1... | collective-permute-start | bytes 49160 | tf_op jit(solution)/shard_map/ppermute | solution.py:18
  622.1 5.0 collective-permute-start.4
  761.8 9.3 copy-start.24
  779.1 18.4 %copy-start.55 = (f32[128]{0:T(128)S(1)}, f32[128]{0:T(128)}, u32[]{:S(2)}) copy-start(f32[128]{0:T(128)} %param.34) | copy-start | bytes 1540
  779.1 18.4 %copy-start.57 = (f32[128]{0:T(128)S(1)}, f32[128]{0:T(128)}, u32[]{:S(2)}) copy-start(f32[128]{0:T(128)} %copy-done.56) | copy-start | bytes 1540
  779.1 19.0 %copy-start.66 = (f32[128]{0:T(128)S(1)}, f32[128]{0:T(128)}, u32[]{:S(2)}) copy-start(f32[128]{0:T(128)} %get-tuple-element.470) | copy-start | bytes 1540
  838.8 179.4 %all-to-all-start.2 = ((bf16[8,1280,128]{2,1,0:T(8,128)(2,1)}), bf16[8,1280,128]{2,1,0:T(8,128)(2,1)}, u32[]{:S(2)}, u32[]{:S(2)}) async-start(bf16[8,1280,128]{2,1,0:T(8,128)(2,1)} %bitcast.430), calls=%async_computation.2 | async-start | bytes 5242880 | tf_op jit(solution)/shard_map/all_to_all | solution.py:374
  843.5 168.0 %all-reduce.6.cloned.1.call-start = ((), (), s32[]{:S(2)}) async-start(), calls=%async_computation.3 | async-start | bytes 2097152 | tf_op jit(solution)/shard_map/psum | solution.py:388
  861.3 156.9 %copy-start.52 = (f32[10240]{0:T(1024)S(1)}, f32[10240]{0:T(1024)}, u32[]{:S(2)}) copy-start(f32[10240]{0:T(1024)} %copy-done.51) | copy-start | bytes 122884
  (65 other events, 208.2 us)
Sparse Core Ops, SparseCore 0:
  861.4 150.0 all-reduce.5
where the time goes:
time: 1090 us; the launch traced here: 1080 us
  matrix products  279 us (26%)
  waiting for transfers between devices  257 us (24%)
  local copies, waits for them, and re-layouts  235 us (22%)
  other arithmetic  200 us (18%)
  blocking collectives  68 us (6%)
  starting transfers between devices  22.2 us (2%)
  between operations  15.6 us (1%)
    psum x1, waiting for transfers between devices, local(): lax.psum((grad_w_vfe, grad_b_vfe, grad_gain_local, grads_zero[0], grads_z...  149 us
    ppermute x5, waiting for transfers between devices, passed_along(): return lax.ppermute(value, axis, pairs)  77.9 us
    dot_general x40, matrix products, block_scores(): jnp.einsum('wqhd,wkhd->whqk', query_blk, key_blk, preferred_element_type=...  72 us
    scatter-add x1, other arithmetic, segment_rows(): jax.ops.segment_sum(hidden_rows, targets, num_segments=slot_count + 1)  67.8 us
    psum x1, blocking collectives, local(): lax.psum((grad_w_vfe, grad_b_vfe, grad_gain_local, grads_zero[0], grads_z...  39.5 us
    gather x1, local copies, waits for them, and re-layouts, local(): point_grad_rows = padded_grad[got_targets]  36.4 us
    dot_general x20, matrix products, one_block(): jnp.einsum('whqk,wkhd->wqhd', grad_scores, key_blk, preferred_element_typ...  33 us
    dynamic_update_slice x40, local copies, waits for them, and re-layouts, attend_forward(): lax.map(one_block, (split_blocks(queries), split_blocks(key_rows), split_...  31.2 us
  transfers between devices with their start and end apart: 9, of which 5 were waited for; matrix products, arithmetic and copies ran while one was open for 47% of the time, Pallas kernels for 0%

commit v1 on v0

v1 whole, which is shorter than its diff:
```python
import functools

import jax
import jax.numpy as jnp
from jax import lax
from jax.experimental import pallas as pl
from jax.experimental.pallas import tpu as pltpu
from jax.sharding import PartitionSpec as P

HEADS = 8
WSLOT = 128
D = 128
FF = 256
HD = D // HEADS
EPS = 1e-05
LOG2E = 1.4426950408889634
GC = 0.7978845608028654
GA = 0.044715
NACC = 8

f32 = jnp.float32
bf16 = jnp.bfloat16
VMEM = pl.BlockSpec(memory_space=pltpu.VMEM)
SMEM = pl.BlockSpec(memory_space=pltpu.SMEM)
VMEM_LIMIT = 56 * 1024 * 1024
MAIN_LIMIT = 62 * 1024 * 1024
GROUP = 10
LATENCY = 120


def dot(a, b):
    return lax.dot_general(a, b, (((1,), (0,)), ((), ())), preferred_element_type=f32)


def dot_nt(a, b):
    return lax.dot_general(a, b, (((1,), (1,)), ((), ())), preferred_element_type=f32)


def dot_tn(a, b):
    return lax.dot_general(a, b, (((0,), (0,)), ((), ())), preferred_element_type=f32)


PQ, PV, PO, PGA, PBA, PI0, PI1, PB, PGF, PBF = range(10)


def layer_scratch():
    return [
        pltpu.VMEM((3 * D, D), bf16),
        pltpu.VMEM((D, D), bf16),
        pltpu.VMEM((FF, D), bf16),
        pltpu.VMEM((D, FF), bf16),
        pltpu.VMEM((10, D, D), f32),
        pltpu.VMEM((HEADS // 2, WSLOT, D), bf16),
    ]


def prepare(layer, w, s):
    w_qkv, b_qv, w_out, b_out, g_at, b_at, w_in, b_in, w_back, b_back, g_ff, b_ff = w
    wqt, wot, wit, wbt, vec, cols = s
    for p in range(HEADS // 2):
        lane = lax.broadcasted_iota(jnp.int32, (WSLOT, D), 1)
        inside = (lane >= 2 * p * HD) & (lane < (2 * p + 2) * HD)
        cols[p] = inside.astype(f32).astype(bf16)
    wqt[0:D, :] = (w_qkv[layer, :, 0:D].astype(f32) * HD ** (-0.5)).T.astype(bf16)
    wqt[D:, :] = w_qkv[layer, :, D:].T
    wot[...] = w_out[layer].T
    wit[...] = w_in[layer].T
    wbt[...] = w_back[layer].T
    sl = slice(layer, layer + 1)
    rows = [
        b_qv[sl, 0:D], b_qv[sl, D : 2 * D], b_out[sl, :], g_at[sl, :], b_at[sl, :],
        b_in[sl, 0:D], b_in[sl, D : 2 * D], b_back[sl, :], g_ff[sl, :], b_ff[sl, :],
    ]
    for i, row in enumerate(rows):
        if i == PQ:
            row = row * HD ** (-0.5)
        vec[i] = jnp.broadcast_to(row, (D, D)).T


NPAIR = HEADS // 2
NQUAD = HEADS // 4
GROW = 64


def cat(xs):
    return jnp.concatenate(xs, axis=1)


def mean0(v):
    return jnp.sum(v, axis=0, keepdims=True) * (1.0 / D)


def norm0(v):
    c = v - mean0(v)
    rs = lax.rsqrt(mean0(c * c) + EPS)
    return c * rs, rs


def norm0_back(gy, xh, rs):
    return rs * (gy - mean0(gy) - xh * mean0(gy * xh))


def gelu(x):
    return x * (0.5 + 0.5 * jnp.tanh(x * (GC + (GC * GA) * (x * x))))


def gelu_low(x):
    u = x * x
    t = jnp.tanh((x * (GC + (GC * GA) * u)).astype(bf16))
    xb, ub = x.astype(bf16), u.astype(bf16)
    h = bf16(0.5) + bf16(0.5) * t
    act = xb * h
    grad = h + act * ((bf16(1.0) - h) * (bf16(2.0 * GC) + bf16(6.0 * GC * GA) * ub))
    return act, grad


def window_masks(shifted, lens, win):
    lane = lax.broadcasted_iota(jnp.int32, (1, WSLOT), 1)
    sub = lax.broadcasted_iota(jnp.int32, (WSLOT, D), 0)
    half = WSLOT // 2
    if shifted:
        first, second = lens(win) - half, lens(win + 1) + half
        ml = lane < jnp.where(lane < half, first, second)
        ms = sub < jnp.where(sub < half, first, second)
    else:
        ml = lane < lens(win)
        ms = sub < lens(win)
    return ml.astype(f32), ms


def head_diag(a, b):
    zero = jnp.zeros((HD, WSLOT), a.dtype)
    return jnp.concatenate([cat([a, zero]), cat([zero, b])], axis=0)


def two_blocks(a, b):
    zero = jnp.zeros(a.shape, a.dtype)
    return jnp.concatenate([cat([a, zero]), cat([zero, b])], axis=0)


def quad_diag(o, ml):
    return jnp.concatenate([o[0 : 2 * HD, 0:WSLOT] * ml, o[2 * HD :, WSLOT:] * ml], axis=0)


def even_odd(heads):
    zero = jnp.zeros((HD, WSLOT), heads[0].dtype)
    return jnp.concatenate(
        [cat([zero, t] if h % 2 else [t, zero]) for h, t in enumerate(heads)], axis=0
    )


def pair_lhs(t, cols):
    return jnp.concatenate([t * cols[p] for p in range(NPAIR)], axis=0)


def head_rows(t):
    return [t[h * HD : (h + 1) * HD] for h in range(HEADS)]


def pair_rows(t, p):
    return t[2 * p * HD : (2 * p + 1) * HD], t[(2 * p + 1) * HD : (2 * p + 2) * HD]


class Values:
    def __init__(self):
        self.d = {}

    def put(self, name, i, value):
        self.d[name, i] = value

    def get(self, name, i):
        return self.d[name, i]


STASH = {
    "xb": (20, (D, 2 * WSLOT), bf16),
    "nb": (20, (D, 2 * WSLOT), bf16),
    "q": (40, (D, WSLOT), bf16),
    "k": (40, (D, WSLOT), bf16),
    "v": (40, (D, WSLOT), bf16),
    "mix": (40, (D, WSLOT), f32),
    "xh1": (40, (D, WSLOT), f32),
    "xh2": (40, (D, WSLOT), f32),
    "dg": (40, (FF, WSLOT), bf16),
    "ia": (40, (FF, WSLOT), bf16),
    "e": (80, (2 * WSLOT, 2 * WSLOT), bf16),
    "rden": (20, (8, 2 * WSLOT), f32),
    "rs1": (20, (8, WSLOT), f32),
    "rs2": (20, (8, WSLOT), f32),
}
ROWS_OF_ONE = ("rden", "rs1", "rs2")


def stash_scratch(nw):
    return [pltpu.VMEM((n * nw // 40, *s), t) for n, s, t in STASH.values()]


class Stash:
    def __init__(self, refs, pair):
        self.refs = dict(zip(STASH, refs))
        self.pair = pair

    def at(self, name, i):
        count = STASH[name][0] // 20
        ref = self.refs[name]
        if name in ROWS_OF_ONE:
            return ref, (self.pair, slice(i, i + 1), slice(None))
        return ref, (self.pair * count + i,)

    def put(self, name, i, value):
        ref, at = self.at(name, i)
        ref[at] = value

    def get(self, name, i):
        ref, at = self.at(name, i)
        return ref[at]


def interleave(gens):
    free = {"m": 0, "v": 0}
    ready = [0] * len(gens)
    ahead = {}
    for c, gen in enumerate(gens):
        ahead[c] = next(gen)
    while ahead:
        c = min(ahead, key=lambda i: (max(free[ahead[i][0]], ready[i]), i))
        kind, cost = ahead[c]
        start = max(free[kind], ready[c])
        free[kind] = start + cost
        ready[c] = start + cost + (LATENCY if kind == "m" else LATENCY // 4)
        try:
            ahead[c] = next(gens[c])
        except StopIteration:
            del ahead[c]


def forward(xs, masks, row0, s, keep):
    wqt, wot, wit, wbt, vec, cols = s
    two = range(2)
    yield "m", 96
    xb = cat(xs).astype(bf16)
    keep.put("xb", 0, xb)
    packed = dot(wqt[...], xb)
    kns, ones, qs, vs = [], [], [], []
    for i in two:
        yield "v", 45
        ml, ms = masks[i]
        pk = packed[:, i * WSLOT : (i + 1) * WSLOT]
        q = (pk[0:D] + vec[PQ]).astype(bf16)
        kf = pk[D : 2 * D] * (ml * LOG2E)
        v = ((pk[2 * D :] + vec[PV]) * ml).astype(bf16)
        k = kf.astype(bf16)
        kn = k.T.astype(f32)
        kn = jnp.where(ms, kn, jnp.broadcast_to(kn[row0 : row0 + 1, :], kn.shape))
        kns.append(kn.astype(bf16))
        mrow = jnp.broadcast_to(ml, (8, WSLOT))
        mzero = jnp.zeros((8, WSLOT), f32)
        ones.append(
            jnp.concatenate([cat([mrow, mzero]), cat([mzero, mrow])], axis=0).astype(bf16)
        )
        qs.append(q)
        vs.append(v)
        keep.put("q", i, q)
        keep.put("k", i, k)
        keep.put("v", i, v)
    items = [(i, u) for i in two for u in range(NQUAD)]
    scores, exps, mixes = {}, {}, {}

    def weigh(t):
        i, u = items[t]
        v4 = vs[i][u * 4 * HD : (u + 1) * 4 * HD]
        lhs = jnp.concatenate([two_blocks(v4[0 : 2 * HD], v4[2 * HD :]), ones[i]], axis=0)
        o = dot(lhs, exps.pop(t))
        parts = []
        for p in range(2):
            den = o[4 * HD + 8 * p : 4 * HD + 8 * p + 1, :]
            rden = 1.0 / den
            keep.put("rden", 2 * t + p, rden)
            rows = o[2 * p * HD : (2 * p + 2) * HD]
            parts += [rows[0:HD, 0:WSLOT] * rden[:, 0:WSLOT], rows[HD:, WSLOT:] * rden[:, WSLOT:]]
        mixes[t] = jnp.concatenate(parts, axis=0)

    for t, (i, u) in enumerate(items):
        if u == 0:
            yield "m", 128
            scores[i] = dot(pair_lhs(kns[i], cols), even_odd(head_rows(qs[i])))
        es = []
        for p in (2 * u, 2 * u + 1):
            yield "v", 35
            sc = scores[i][p * WSLOT : (p + 1) * WSLOT]
            es.append(jnp.exp2((sc - jnp.max(sc, axis=0, keepdims=True)).astype(bf16)))
        exps[t] = jnp.concatenate(es, axis=0)
        keep.put("e", t, exps[t])
        yield "m", 64
        weigh(t)
    mix = [jnp.concatenate([mixes[i * NQUAD + u] for u in range(NQUAD)], axis=0) for i in two]
    for i in two:
        keep.put("mix", i, mix[i])
    yield "m", 32
    branch = dot(wot[...], cat(mix).astype(bf16))
    normed = []
    for i in two:
        yield "v", 50
        first = xs[i] + (branch[:, i * WSLOT : (i + 1) * WSLOT] + vec[PO])
        xh, rs = norm0(first)
        keep.put("xh1", i, xh)
        keep.put("rs1", i, rs)
        normed.append(xh * vec[PGA] + vec[PBA])
    yield "m", 64
    nb = cat(normed).astype(bf16)
    keep.put("nb", 0, nb)
    pre = dot(wit[...], nb)
    inner = []
    for i in two:
        acts, grads = [], []
        for r in range(0, FF, GROW):
            if r % (2 * GROW) == 0:
                yield "v", 50
            bias = vec[PI0 + r // D, r % D : r % D + GROW, :]
            act, grad = gelu_low(pre[r : r + GROW, i * WSLOT : (i + 1) * WSLOT] + bias)
            acts.append(act)
            grads.append(grad)
        inner.append(jnp.concatenate(acts, axis=0))
        keep.put("ia", i, inner[i])
        keep.put("dg", i, jnp.concatenate(grads, axis=0))
    yield "m", 64
    outer = dot(wbt[...], cat(inner))
    out = []
    for i in two:
        yield "v", 55
        second = normed[i] + (outer[:, i * WSLOT : (i + 1) * WSLOT] + vec[PB])
        xh, rs = norm0(second)
        keep.put("xh2", i, xh)
        keep.put("rs2", i, rs)
        out.append((xh * vec[PGF] + vec[PBF]) * masks[i][0])
    return out


def backward(des, masks, layer, w, s, acc, keep):
    w_qkv, w_out, w_in, w_back = w[0], w[2], w[6], w[8]
    a_qkv, a_out, a_in, a_back, a_vec = acc
    vec, cols = s[4:6]
    two = range(2)
    ones = jnp.ones((16, 2 * WSLOT), bf16)
    d_second = []
    for i in two:
        yield "v", 65
        dy = des[i] * masks[i][0]
        xh = keep.get("xh2", i)
        a_vec[0] += dy * xh
        a_vec[1] += dy
        d_second.append(norm0_back(dy * vec[PGF], xh, keep.get("rs2", i)))
    yield "m", 64
    do = cat(d_second).astype(bf16)
    d_act = dot(w_back[layer], do)
    yield "m", 64
    inner = cat([keep.get("ia", i) for i in two])
    a_back[...] += dot_nt(jnp.concatenate([inner, ones], axis=0), do)
    dis = []
    for i in two:
        yield "v", 25
        d = d_act[:, i * WSLOT : (i + 1) * WSLOT].astype(bf16)
        dis.append(keep.get("dg", i) * d)
    yield "m", 64
    di = cat(dis)
    dn = dot(w_in[layer], di)
    yield "m", 64
    a_in[...] += dot_nt(jnp.concatenate([keep.get("nb", 0), ones], axis=0), di)
    d_first = []
    for i in two:
        yield "v", 70
        d = d_second[i] + dn[:, i * WSLOT : (i + 1) * WSLOT]
        xh = keep.get("xh1", i)
        a_vec[2] += d * xh
        a_vec[3] += d
        d_first.append(norm0_back(d * vec[PGA], xh, keep.get("rs1", i)))
    yield "m", 32
    db = cat(d_first).astype(bf16)
    dm = dot(w_out[layer], db)
    yield "m", 64
    mixb = cat([keep.get("mix", i) for i in two]).astype(bf16)
    a_out[...] += dot_nt(jnp.concatenate([mixb, ones], axis=0), db)
    items = [(i, u) for i in two for u in range(NQUAD)]
    dps, dms, rowdots, dqs, dks, dvs = {}, {}, {}, {}, {}, {}
    for t, (i, u) in enumerate(items):
        if u == 0:
            yield "v", 25
            heads, dots = [], []
            grad = head_rows(dm[:, i * WSLOT : (i + 1) * WSLOT])
            mix = head_rows(keep.get("mix", i))
            for h in range(HEADS):
                rden = keep.get("rden", i * NPAIR + h // 2)
                d = grad[h] * rden[:, (h % 2) * WSLOT : (h % 2 + 1) * WSLOT]
                dots.append(jnp.sum(d * mix[h], axis=0, keepdims=True))
                heads.append(d.astype(bf16))
            dms[i], rowdots[i] = heads, dots
            yield "m", 128
            dps[i] = dot(pair_lhs(keep.get("v", i).T, cols), even_odd(heads))
        yield "m", 64
        e = keep.get("e", t)
        heads = dms[i][4 * u : 4 * u + 4]
        dd = jnp.concatenate([head_diag(*heads[0:2]), head_diag(*heads[2:4])], axis=0)
        dvs[t] = quad_diag(dot_nt(dd, e), masks[i][0])
        ds = []
        for p in range(2):
            yield "v", 25
            h = 4 * u + 2 * p
            dp = dps[i][(2 * u + p) * WSLOT : (2 * u + p + 1) * WSLOT]
            rowdot = cat(rowdots[i][h : h + 2])
            ds.append(e[p * WSLOT : (p + 1) * WSLOT] * (dp - rowdot).astype(bf16))
        ds = jnp.concatenate(ds, axis=0)
        yield "m", 64
        k4 = keep.get("k", i)[u * 4 * HD : (u + 1) * 4 * HD]
        o = dot(two_blocks(k4[0 : 2 * HD], k4[2 * HD :]), ds)
        o = [o[j * HD : (j + 1) * HD, (j % 2) * WSLOT : (j % 2 + 1) * WSLOT] for j in range(4)]
        dqs[t] = jnp.concatenate(o, axis=0) * (HD ** (-0.5) / LOG2E)
        yield "m", 64
        heads = head_rows(keep.get("q", i))[4 * u : 4 * u + 4]
        q = jnp.concatenate([head_diag(*heads[0:2]), head_diag(*heads[2:4])], axis=0)
        dks[t] = quad_diag(dot_nt(q, ds), masks[i][0])

    def whole(d):
        return cat(
            [jnp.concatenate([d[i * NQUAD + u] for u in range(NQUAD)], axis=0) for i in two]
        ).astype(bf16)

    yield "m", 96
    dpk = jnp.concatenate([whole(dqs), whole(dks), whole(dvs)], axis=0)
    dx = dot(w_qkv[layer], dpk)
    yield "m", 128
    a_qkv[...] += dot_nt(jnp.concatenate([keep.get("xb", 0), ones], axis=0), dpk)
    yield "v", 20
    return [d_first[i] + dx[:, i * WSLOT : (i + 1) * WSLOT] for i in two]


ACC_SHAPES = [(D + 16, 3 * D), (D + 16, D), (D + 16, FF), (FF + 16, D), (4, D, D)]


def clear(acc):
    for a in acc:
        a[...] = jnp.zeros(a.shape, f32)


def shift_tile(left, right):
    half = WSLOT // 2
    lane = lax.broadcasted_iota(jnp.int32, left.shape, 1)
    return pltpu.roll(jnp.where(lane < half, right, left), half, 1)


def encoded_pair(ps, coef, w0):
    out = []
    for i in range(2):
        at = pl.ds(pl.multiple_of((w0 + i) * WSLOT, WSLOT), WSLOT)
        out.append((ps[at, :] * coef).T)
    return out


def first_forward_step(g, w0, lens, ps, coef, tiles, s, stash):
    def chain(c):
        w = w0 + 2 * c
        masks = [window_masks(False, lens, w + i) for i in range(2)]
        keep = Values() if stash is None else Stash(stash, w // 2)
        out = yield from forward(encoded_pair(ps, coef, w), masks, 0, s, keep)
        for i in range(2):
            tiles[w + i] = out[i]

    interleave([chain(c) for c in range(g // 2)])


def second_step(g, w0, lens, tiles, cots, out_rows, gv, gv0, w, s, acc):
    def chain(c):
        v = w0 + 2 * c
        masks = [window_masks(True, lens, v + i) for i in range(2)]
        ts = [tiles[v + i] for i in range(3)]
        xs = [shift_tile(ts[i], ts[i + 1]) for i in range(2)]
        keep = Values()
        out = yield from forward(xs, masks, WSLOT // 2, s, keep)
        for i in range(2):
            out_rows(v + i, out[i].astype(bf16).T)
        des = [cots(v + i).T.astype(f32) for i in range(2)]
        dx = yield from backward(des, masks, 1, w, s, acc, keep)
        for i in range(2):
            gv[gv0 + v + i] = dx[i]

    interleave([chain(c) for c in range(g // 2)])


def first_backward_step(g, w0, lens, ps, coef, gv, put_grad, w, s, acc, stash):
    def chain(c):
        v = w0 + 2 * c
        masks = [window_masks(False, lens, v + i) for i in range(2)]
        if stash is None:
            keep = Values()
            yield from forward(encoded_pair(ps, coef, v), masks, 0, s, keep)
        else:
            keep = Stash(stash, v // 2)
        ts = [gv[v + i] for i in range(3)]
        des = [shift_tile(ts[i], ts[i + 1]) for i in range(2)]
        dx = yield from backward(des, masks, 0, w, s, acc, keep)
        for i in range(2):
            put_grad(v + i, dx[i].T)

    interleave([chain(c) for c in range(g // 2)])


def row_block(ref, start):
    return ref[pl.ds(pl.multiple_of(start, WSLOT // 2), WSLOT), :]


def first_forward_kernel(nw, g, lens, ps, coef, *refs):
    w, out, s = refs[:12], refs[12], refs[13:]
    prepare(0, w, s)

    def body(j, _):
        first_forward_step(g, g * j, lambda i: lens[i], ps, coef[...], out, s, None)
        return 0

    lax.fori_loop(0, nw // g, body, 0)


def second_kernel(nw, g, lens, fo, rim, cot, rim_cot, *refs):
    w = refs[:12]
    out, gv = refs[12:14]
    acc = refs[14:19]
    s = refs[19:25]
    tiles, cots = refs[25:27]
    prepare(1, w, s)
    clear(acc)
    half = WSLOT // 2
    tiles[0:nw] = fo[...]
    tiles[nw] = rim[...].astype(f32)
    n = nw * WSLOT
    cots[0 : n - half, :] = cot[half:, :]
    cots[n - half :, :] = rim_cot[...]

    def put(win, rows):
        out[pl.ds(pl.multiple_of(win * WSLOT, WSLOT), WSLOT), :] = rows

    def body(j, _):
        second_step(
            g, g * j, lambda i: lens[i], tiles, lambda i: row_block(cots, i * WSLOT), put, gv, 0,
            w, s, acc,
        )
        return 0

    lax.fori_loop(0, nw // g, body, 0)


def first_backward_kernel(nw, g, lens, ps, coef, gv, back, *refs):
    w = refs[:12]
    d_enc = refs[12]
    acc = refs[13:18]
    s = refs[18:24]
    tiles = refs[24]
    prepare(0, w, s)
    clear(acc)
    tiles[1 : nw + 1] = gv[...]
    tiles[0] = back[...].astype(f32)

    def put_grad(win, rows):
        d_enc[pl.ds(pl.multiple_of(win * WSLOT, WSLOT), WSLOT), :] = rows

    def body(j, _):
        first_backward_step(
            g, g * j, lambda i: lens[i], ps, coef[...], tiles, put_grad, w, s, acc, None
        )
        return 0

    lax.fori_loop(0, nw // g, body, 0)


def chunks(bucket):
    step = 2 * D if bucket % (2 * D) == 0 else bucket
    return [slice(c, c + step) for c in range(0, bucket, step)]


def scatter_kernel(nw, slots, lens, feats, w, b, ps, stat, hid, *accs):
    tiles, _, bucket = feats.shape
    pitch = slots.shape[0] // tiles
    rows = accs[0].shape[0]

    def zero(i, _):
        for a in accs:
            a[pl.ds(pl.multiple_of(i * 128, 128), 128), :] = jnp.zeros((128, D), f32)
        return 0

    lax.fori_loop(0, rows // 128, zero, 0)

    def one_bucket(t, _):
        parts = chunks(bucket)
        pres = [dot_tn(feats[t, :, at], w[...]) for at in parts]
        for at, pre in zip(parts, pres):
            hid[at, :] = gelu(pre + b[...])

        def some(i, _):
            base = i * 8
            for u in range(0, 8, NACC // 2):
                at, h = [], []
                for a in range(NACC // 2):
                    for far, r in enumerate(both_slots(slots[t * pitch + base + u + a])):
                        at.append(pl.ds(r, 1))
                        h.append(hid[pl.ds(far * (bucket // 2) + base + u + a, 1), :])
                new = [accs[a][at[a], :] + h[a] for a in range(NACC)]
                for a in range(NACC):
                    accs[a][at[a], :] = new[a]
            return 0

        lax.fori_loop(0, bucket // 16, some, 0)
        return 0

    lax.fori_loop(0, tiles, one_bucket, 0)

    sub = lax.broadcasted_iota(jnp.int32, (WSLOT, D), 0)

    def finish(j, carry):
        sq, cnt = carry
        for win in range(2):
            win = 2 * j + win
            at = pl.ds(pl.multiple_of(win * WSLOT, WSLOT), WSLOT)
            total = accs[0][at, :]
            for a in accs[1:]:
                total = total + a[at, :]
            ps[at, :] = total
            valid = (sub < lens[0, win]).astype(f32)
            sq, cnt = sq + valid * total * total, cnt + valid
        return sq, cnt

    z = jnp.zeros((WSLOT, D), f32)
    sq, cnt = lax.fori_loop(0, nw // 2, finish, (z, z))
    stat[...] = jnp.zeros(stat.shape, f32)
    stat[0:1, :] = jnp.sum(sq, axis=0, keepdims=True)
    stat[1:2, :] = jnp.sum(cnt, axis=0, keepdims=True)


def point_bucket(t, slots, feats, w, b, dp, got, put, gw, gb):
    tiles, _, bucket = feats.shape
    pitch = slots.shape[0] // tiles

    def some(i, _):
        for base in range(0, 32, 16):
            at = i * 32 + base
            words = [both_slots(slots[t * pitch + at + u]) for u in range(16)]
            new = [dp[pl.ds(r, 1), :] for word in words for r in word]
            for u in range(16):
                for far in range(2):
                    got[pl.ds(far * (bucket // 2) + at + u, 1), :] = new[2 * u + far]
        return 0

    lax.fori_loop(0, bucket // 64, some, 0)
    for u in range(bucket // 64 * 32, bucket // 2):
        for far, row in enumerate(both_slots(slots[t * pitch + u])):
            at = far * (bucket // 2) + u
            got[at : at + 1, :] = dp[pl.ds(row, 1), :]

    parts = chunks(bucket)
    fts = [feats[t, :, at] for at in parts]
    pres = [dot_tn(ft, w[...]) for ft in fts]
    dpres = [
        gelu_low(pre + b[...])[1] * got[at, :].astype(bf16) for at, pre in zip(parts, pres)
    ]
    for at, dpre in zip(parts, dpres):
        put(t, at, dot_nt(w[...], dpre).astype(bf16))
    total = dot(fts[0], dpres[0])
    for ft, dpre in zip(fts[1:], dpres[1:]):
        total = total + dot(ft, dpre)
    gw[...] += total
    for dpre in dpres:
        gb[...] += jnp.sum(dpre.astype(f32).reshape(dpre.shape[0] // 8, 8, D), axis=0)


def gather_kernel(nw, slots, lens, feats, w, b, d_enc, ps, ca, cb, out, gw, gb, dp, got):
    tiles, _, bucket = feats.shape
    sub = lax.broadcasted_iota(jnp.int32, (WSLOT, D), 0)

    def make(win, _):
        at = pl.ds(pl.multiple_of(win * WSLOT, WSLOT), WSLOT)
        valid = (sub < lens[0, win]).astype(f32)
        dp[at, :] = d_enc[at, :] * ca[...] - ps[at, :] * valid * cb[...]
        return 0

    lax.fori_loop(0, nw, make, 0)
    dp[nw * WSLOT : nw * WSLOT + 128, :] = jnp.zeros((128, D), f32)
    gw[...] = jnp.zeros(gw.shape, f32)
    gb[...] = jnp.zeros(gb.shape, f32)

    def put(t, at, rows):
        out[t, :, at] = rows

    def one_bucket(t, _):
        point_bucket(t, slots, feats, w, b, dp, got, put, gw, gb)
        return 0

    lax.fori_loop(0, tiles, one_bucket, 0)


EXTRA = 64
VFE_ROW = 32
MESH = pl.DeviceIdType.MESH


def peers(axis, count):
    me = lax.axis_index(axis)
    return me, [lax.rem(me + d, count) for d in range(1, count)]


def remote(src, dst, send, recv, axis, peer):
    return pltpu.make_async_remote_copy(
        src_ref=src, dst_ref=dst, send_sem=send, recv_sem=recv,
        device_id={axis: peer}, device_id_type=MESH,
    )


def far_first(d, count):
    near = lax.div(d + 1, 2)
    return lax.rem(count // 2 + jnp.where(lax.rem(d, 2) == 0, near, count - near), count)


def start_all(copies):
    for c in copies:
        c.start()


def wait_all(copies):
    for c in copies:
        c.wait()


def greet(axes):
    barrier = pltpu.get_barrier_semaphore()
    for axis, count in axes:
        for peer in peers(axis, count)[1]:
            pl.semaphore_signal(barrier, 1, device_id={axis: peer}, device_id_type=MESH)
    pl.semaphore_wait(barrier, sum(count - 1 for _, count in axes))


def blocks(acc):
    a_qkv, a_out, a_in, a_back, _ = acc
    return (
        [a_qkv[0:D, i * D : (i + 1) * D] for i in range(3)]
        + [a_out[0:D, :]]
        + [a_in[0:D, i * D : (i + 1) * D] for i in range(2)]
        + [a_back[i * D : (i + 1) * D, :] for i in range(2)]
    )


class Reducer:
    ROWS = 8 * D

    def __init__(self, frames, tiles, refs, full):
        self.frames, self.tiles, self.full = frames, tiles, full
        self.mine, self.got1, self.part, self.got2, self.ss, self.rs = refs
        self.me_f, self.peers_f = peers("frame", frames)
        self.me_t, self.peers_t = peers("tile", tiles)
        per = self.part.shape[1]
        self.here = pl.ds(pl.multiple_of(self.me_t * per, per), per)

    @staticmethod
    def scratch(frames, tiles):
        per_f = Reducer.ROWS // frames
        per_t = per_f // tiles
        count = 2 * (frames - 1) + 2 * (tiles - 1)
        return [
            pltpu.VMEM((frames, per_f, D), bf16),
            pltpu.VMEM((frames - 1, per_f, D), bf16),
            pltpu.VMEM((tiles, per_t, D), bf16),
            pltpu.VMEM((tiles - 1, per_t, D), bf16),
            pltpu.SemaphoreType.DMA((count,)),
            pltpu.SemaphoreType.DMA((count,)),
        ]

    def copies(self, stage):
        axis = "frame" if stage in (0, 3) else "tile"
        prs = self.peers_f if axis == "frame" else self.peers_t
        f, t = self.frames - 1, self.tiles - 1
        at = (0, f, f + t, f + 2 * t)[stage]
        out = []
        for i, p in enumerate(prs):
            if stage == 0:
                src, dst = self.mine.at[p], self.got1.at[i]
            elif stage == 1:
                src, dst = self.part.at[p], self.got2.at[i]
            elif stage == 2:
                src = dst = self.full.at[self.me_f, self.here, :]
            else:
                src = dst = self.full.at[self.me_f]
            out.append(remote(src, dst, self.ss.at[at + i], self.rs.at[at + i], axis, p))
        return out

    def step1(self, acc):
        per = self.mine.shape[1]
        for i, block in enumerate(blocks(acc)):
            r = i * D
            self.mine[r // per, r % per : r % per + D, :] = block.astype(bf16)
        start_all(self.copies(0))

    def step2(self):
        wait_all(self.copies(0))
        total = self.mine[self.me_f].astype(f32)
        for i in range(self.frames - 1):
            total = total + self.got1[i].astype(f32)
        self.part[...] = total.astype(bf16).reshape(self.part.shape)
        start_all(self.copies(1))

    def step3(self):
        wait_all(self.copies(1))
        total = self.part[self.me_t].astype(f32)
        for i in range(self.tiles - 1):
            total = total + self.got2[i].astype(f32)
        self.full[self.me_f, self.here, :] = total.astype(bf16)
        start_all(self.copies(2))

    def step4(self):
        wait_all(self.copies(2))
        start_all(self.copies(3))

    def step5(self):
        wait_all(self.copies(3))


def extra_rows(acc):
    a_qkv, a_out, a_in, a_back, a_vec = acc
    r = [a_qkv[D : D + 1, i * D : (i + 1) * D] for i in range(3)]
    r.append(a_out[D : D + 1, :])
    r += [jnp.sum(a_vec[i].T, axis=0, keepdims=True) for i in (2, 3)]
    r += [a_in[D : D + 1, i * D : (i + 1) * D] for i in range(2)]
    r.append(a_back[FF : FF + 1, :])
    r += [jnp.sum(a_vec[i].T, axis=0, keepdims=True) for i in (0, 1)]
    r.append(jnp.zeros((5, D), f32))
    return jnp.concatenate(r, axis=0)


def slot_rows(bucket):
    return -(-bucket // (16 * D)) * 8


def both_slots(word):
    return word & 0xFFFF, lax.shift_right_logical(word, 16)


def exchange_kernel(tiles, n, blen, wlen, slot, feats, got_feats, got_slots, next_len, *scr):
    fbuf, tslot, lbuf, ss, rs, ss2, rs2, ss3, rs3 = scr
    bucket = fbuf.shape[2]
    me, prs = peers("tile", tiles)
    for t in range(tiles):
        fbuf[t] = feats[0, :, t * bucket : (t + 1) * bucket]
    greet((("tile", tiles),))
    points = [
        remote(fbuf.at[p], got_feats.at[me], ss.at[i], rs.at[i], "tile", p)
        for i, p in enumerate(prs)
    ]
    order = sorted(range(tiles - 1), key=lambda i: abs(2 * (i + 1) - tiles))
    start_all([points[i] for i in order])
    lane = lax.broadcasted_iota(jnp.int32, (1, D), 1)
    rows = tslot.shape[1]
    for t in range(tiles):
        parts = [
            jnp.where(lane + c < blen[0, t], slot[:, t * bucket + c : t * bucket + c + D], n)
            for c in range(0, bucket, D)
        ]
        half = len(parts) // 2
        parts = [a + b * 65536 for a, b in zip(parts[:half], parts[half:])]
        parts.append(jnp.full((rows - half, D), n, jnp.int32))
        tslot[t] = jnp.concatenate(parts, axis=0)
    slots = [
        remote(tslot.at[p], got_slots.at[me], ss2.at[i], rs2.at[i], "tile", p)
        for i, p in enumerate(prs)
    ]
    start_all([slots[i] for i in order])
    lbuf[...] = jnp.full(lbuf.shape, wlen[0, 0], jnp.int32)
    lens = remote(lbuf, next_len, ss3.at[0], rs3.at[0], "tile", lax.rem(me + tiles - 1, tiles))
    lens.start()
    got_feats[me] = fbuf[me]
    got_slots[me] = tslot[me]
    wait_all(points + slots + [lens])


def main_scratch(frames, tiles, nw, pf, bucket):
    n = nw * WSLOT
    half = WSLOT // 2
    dma = pltpu.SemaphoreType.DMA
    return {
        "s0": layer_scratch(),
        "s1": layer_scratch(),
        "a0": [pltpu.VMEM(a, f32) for a in ACC_SHAPES],
        "a1": [pltpu.VMEM(a, f32) for a in ACC_SHAPES],
        "stash": stash_scratch(nw),
        "tiles": [pltpu.VMEM((nw + 1, D, WSLOT), f32)],
        "gv": [pltpu.VMEM((nw + 1, D, WSLOT), f32)],
        "rim": [pltpu.VMEM((D, WSLOT), bf16)] * 4,
        "po": [pltpu.VMEM((n + half, D), bf16)],
        "cot": [pltpu.VMEM((n + half, D), bf16)],
        "dp": [pltpu.VMEM((n + WSLOT, D), f32)],
        "dot": [pltpu.VMEM((WSLOT, D), f32)],
        "got": [pltpu.VMEM((bucket, D), f32)],
        "gout": [pltpu.VMEM((tiles, pf, bucket), bf16)],
        "gw": [pltpu.VMEM((pf, D), f32), pltpu.VMEM((8, D), f32)],
        "xstat": [pltpu.VMEM((tiles, 8, D), f32), dma((tiles - 1,)), dma((tiles - 1,))],
        "xdot": [pltpu.VMEM((tiles, 8, D), f32), dma((tiles - 1,)), dma((tiles - 1,))],
        "rsem": [dma((4,)), dma((4,))],
        "gsem": [dma((tiles - 1,)), dma((tiles - 1,))],
        "own": [dma((3,))],
        "r0": Reducer.scratch(frames, tiles),
        "r1": Reducer.scratch(frames, tiles),
        "x0": FrameTile.scratch(frames, tiles, VFE_ROW),
        "x1": FrameTile.scratch(frames, tiles, 24),
    }


def split_refs(spec, refs):
    out, at = {}, 0
    for name, entries in spec.items():
        out[name] = refs[at : at + len(entries)]
        at += len(entries)
    return out


class FrameTile:
    def __init__(self, frames, tiles, refs):
        self.x1, self.x2, self.ss, self.rs = refs
        self.frames, self.tiles = frames, tiles
        self.me_f, self.prs_f = peers("frame", frames)
        self.me_t, self.prs_t = peers("tile", tiles)

    @staticmethod
    def scratch(frames, tiles, rows):
        count = frames + tiles - 2
        return [
            pltpu.VMEM((frames, rows, D), f32), pltpu.VMEM((tiles, rows, D), f32),
            pltpu.SemaphoreType.DMA((count,)), pltpu.SemaphoreType.DMA((count,)),
        ]

    def copies(self, axis):
        if axis == "frame":
            at, view, prs = 0, self.x1.at[self.me_f], self.prs_f
        else:
            at, view, prs = self.frames - 1, self.x2.at[self.me_t], self.prs_t
        return [
            remote(view, view, self.ss.at[at + i], self.rs.at[at + i], axis, p)
            for i, p in enumerate(prs)
        ]

    def start(self, value):
        self.x1[self.me_f] = value
        start_all(self.copies("frame"))

    def middle(self):
        wait_all(self.copies("frame"))
        total = self.x1[0]
        for f in range(1, self.frames):
            total = total + self.x1[f]
        self.x2[self.me_t] = total
        start_all(self.copies("tile"))

    def total(self):
        wait_all(self.copies("tile"))
        total = self.x2[0]
        for t in range(1, self.tiles):
            total = total + self.x2[t]
        return total


class All:
    def __init__(self, tiles, refs):
        self.buf, self.ss, self.rs = refs
        self.tiles = tiles
        self.me, self.prs = peers("tile", tiles)

    def copies(self):
        view = self.buf.at[self.me]
        return [
            remote(view, view, self.ss.at[i], self.rs.at[i], "tile", p)
            for i, p in enumerate(self.prs)
        ]

    def start(self, value):
        self.buf[self.me] = value
        start_all(self.copies())

    def total(self):
        wait_all(self.copies())
        total = self.buf[0]
        for t in range(1, self.tiles):
            total = total + self.buf[t]
        return total


def main_kernel(frames, tiles, nw, g, spec, *refs):
    slots, wlen, next_len, cot, stat, ps, feats, w_vfe, b_vfe, gain = refs[:10]
    w = refs[10:22]
    pillar_out, gp, full0, full1, small = refs[22:27]
    r = split_refs(spec, refs[27:])
    n = nw * WSLOT
    half = WSLOT // 2
    bucket = feats.shape[2]
    pitch = slots.shape[0] // tiles
    groups = nw // g
    me_t, prs_t = peers("tile", tiles)
    me_f, prs_f = peers("frame", frames)
    before, after = lax.rem(me_t + tiles - 1, tiles), lax.rem(me_t + 1, tiles)
    greet((("frame", frames), ("tile", tiles)))

    (cotx,), (own,) = r["cot"], r["own"]
    stats = All(tiles, r["xstat"])
    stats.start(stat[...])
    rss, rrs = r["rsem"]
    cot_rim = remote(
        cot.at[0, 0:half, :], cotx.at[n : n + half, :], rss.at[0], rrs.at[0], "tile", before
    )
    cot_rim.start()
    cot_own = pltpu.make_async_copy(cot.at[0], cotx.at[0:n, :], own.at[0])
    cot_own.start()
    s0, s1, a0, a1 = r["s0"], r["s1"], r["a0"], r["a1"]
    prepare(0, w, s0)
    prepare(1, w, s1)
    clear(a0)
    clear(a1)
    sums = stats.total()
    count = sums[1:2, :]
    scale = lax.rsqrt(sums[0:1, :] / count + EPS)
    coef = scale * gain[...]

    def lens(i):
        return jnp.where(i < nw, wlen[0, jnp.minimum(i, nw - 1)], next_len[0, 0])

    (fo,), (gv,), (po,) = r["tiles"], r["gv"], r["po"]
    rim_out, rim_in, gv_out, gv_in = r["rim"]

    def rim_copy():
        return remote(rim_out, rim_in, rss.at[1], rrs.at[1], "tile", before)

    def fwd(j, _):
        first_forward_step(g, g * j, lens, ps, coef, fo, s0, r["stash"])

        @pl.when(j == 0)
        def _():
            rim_out[...] = fo[0].astype(bf16)
            rim_copy().start()

        return 0

    lax.fori_loop(0, groups, fwd, 0)
    rim_copy().wait()
    fo[nw] = rim_in[...].astype(f32)
    cot_rim.wait()
    cot_own.wait()

    def gv_copy():
        return remote(gv_out, gv_in, rss.at[2], rrs.at[2], "tile", after)

    def po_copy():
        return remote(
            po.at[n : n + half, :], pillar_out.at[0:half, :], rss.at[3], rrs.at[3], "tile", after
        )

    def put_rows(win, rows):
        po[pl.ds(pl.multiple_of(win * WSLOT + half, half), WSLOT), :] = rows

    def second(j, _):
        w0 = g * lax.rem(j + groups - 1, groups)
        second_step(
            g, w0, lens, fo, lambda i: row_block(cotx, i * WSLOT + half), put_rows, gv, 1,
            w, s1, a1,
        )

        @pl.when(j == 0)
        def _():
            gv_out[...] = gv[nw].astype(bf16)
            gv_copy().start()
            po_copy().start()

        return 0

    lax.fori_loop(0, groups, second, 0)
    po_own = pltpu.make_async_copy(po.at[half:n, :], pillar_out.at[half:n, :], own.at[1])
    po_own.start()
    lay1 = Reducer(frames, tiles, r["r1"], full1)
    lay1.step1(a1)
    gv_copy().wait()
    gv[0] = gv_in[...].astype(f32)
    (dp,), (dot_acc,) = r["dp"], r["dot"]
    dot_acc[...] = jnp.zeros(dot_acc.shape, f32)

    def put_grad(win, rows):
        at = pl.ds(pl.multiple_of(win * WSLOT, WSLOT), WSLOT)
        dp[at, :] = rows
        dot_acc[...] += rows * ps[at, :]

    def bwd(j, _):
        first_backward_step(g, g * j, lens, ps, coef, gv, put_grad, w, s0, a0, r["stash"])
        for at, step in ((1, lay1.step2), (2, lay1.step3), (3, lay1.step4)):
            pl.when(j == at)(step)
        return 0

    lax.fori_loop(0, groups, bwd, 0)

    local_dot = jnp.sum(dot_acc[...], axis=0, keepdims=True)
    dots = All(tiles, r["xdot"])
    dots.start(jnp.broadcast_to(local_dot, (8, D)))
    lay0 = Reducer(frames, tiles, r["r0"], full0)
    lay0.step1(a0)
    early, late = FrameTile(frames, tiles, r["x0"]), FrameTile(frames, tiles, r["x1"])
    early.start(jnp.concatenate([extra_rows(a0), extra_rows(a1)], axis=0))
    (got,), (gout,), (gw, gb) = r["got"], r["gout"], r["gw"]
    gw[...] = jnp.zeros(gw.shape, f32)
    gb[...] = jnp.zeros(gb.shape, f32)
    dp[n:, :] = jnp.zeros((WSLOT, D), f32)
    cb = gain[...] * scale * scale * scale * dots.total()[0:1, :] / count
    sub = lax.broadcasted_iota(jnp.int32, (WSLOT, D), 0)

    def make(j, _):
        for win in range(4):
            win = 4 * j + win
            at = pl.ds(pl.multiple_of(win * WSLOT, WSLOT), WSLOT)
            valid = (sub < wlen[0, win]).astype(f32)
            dp[at, :] = dp[at, :] * coef - ps[at, :] * valid * cb
        return 0

    lax.fori_loop(0, nw // 4, make, 0)

    gss, grs = r["gsem"]
    def place(d):
        return lax.rem(me_t + far_first(d, tiles), tiles)

    def points_copy(d):
        t = place(d)
        return remote(gout.at[t], gp.at[me_t], gss.at[d], grs.at[d], "tile", t)

    def put_points(t, at, rows):
        gout[t, :, at] = rows

    def one_bucket(d, _):
        point_bucket(place(d), slots, feats, w_vfe, b_vfe, dp, got, put_points, gw, gb)

        @pl.when(d < tiles - 1)
        def _():
            points_copy(d).start()

        for at, action in ((2, lay0.step2), (3, early.middle), (4, lay0.step3), (6, lay0.step4)):
            pl.when(d == at)(action)
        return 0

    lax.fori_loop(0, tiles, one_bucket, 0)
    gp_own = pltpu.make_async_copy(gout.at[me_t], gp.at[me_t], own.at[2])
    gp_own.start()

    late.start(
        jnp.concatenate(
            [
                gw[...], jnp.sum(gb[...], axis=0, keepdims=True), local_dot * scale,
                jnp.zeros((6, D), f32),
            ],
            axis=0,
        )
    )
    small[0:VFE_ROW, :] = early.total()
    late.middle()
    lay1.step5()
    lay0.step5()
    po_copy().wait()
    po_own.wait()
    gp_own.wait()
    for d in range(tiles - 1):
        points_copy(d).wait()
    small[VFE_ROW : VFE_ROW + 24, :] = late.total()


def finish_kernel(po, gp, full0, full1, small, *outs):
    (
        o_po, o_gp, g_w_vfe, g_b_vfe, g_gain, g_qkv, g_bqv, g_out, g_bout, g_ga, g_ba, g_in, g_bin,
        g_back, g_bback, g_gf, g_bf,
    ) = outs
    o_po[0] = po[...]
    tiles, _, bucket = gp.shape
    for t in range(tiles):
        o_gp[0, :, t * bucket : (t + 1) * bucket] = gp[t]
    g_w_vfe[...] = small[VFE_ROW : VFE_ROW + 16, :]
    g_b_vfe[...] = small[VFE_ROW + 16 : VFE_ROW + 17, :]
    g_gain[...] = small[VFE_ROW + 17 : VFE_ROW + 18, :]
    for l, full in enumerate((full0, full1)):
        one = slice(l, l + 1)

        def row(i):
            return small[16 * l + i : 16 * l + i + 1, :]

        g_bqv[one, 0:D] = row(0)
        g_bqv[one, D:] = row(2)
        g_bout[one, :] = row(3)
        g_ga[one, :] = row(4)
        g_ba[one, :] = row(5)
        g_bin[one, 0:D] = row(6)
        g_bin[one, D:] = row(7)
        g_bback[one, :] = row(8)
        g_gf[one, :] = row(9)
        g_bf[one, :] = row(10)
        per = full.shape[1]

        def block(i):
            r = i * D
            return full[r // per, r % per : r % per + D, :].astype(f32)

        for i in range(3):
            g_qkv[l, :, i * D : (i + 1) * D] = block(i)
        g_out[l] = block(3)
        for i in range(2):
            g_in[l, :, i * D : (i + 1) * D] = block(4 + i)
            g_back[l, i * D : (i + 1) * D, :] = block(6 + i)


def shape(s, t):
    return jax.ShapeDtypeStruct(s, t)


def call(kernel, out_shape, n_smem, n_in, scratch, *args):
    return pl.pallas_call(
        kernel,
        out_shape=out_shape,
        in_specs=[SMEM] * n_smem + [VMEM] * (n_in - n_smem),
        out_specs=jax.tree.map(lambda _: VMEM, out_shape),
        scratch_shapes=scratch,
        compiler_params=pltpu.CompilerParams(vmem_limit_bytes=VMEM_LIMIT),
    )(*args)


def passed_along(value, axis, steps):
    count = lax.axis_size(axis)
    return lax.ppermute(value, axis, [(i, (i + steps) % count) for i in range(count)])


def unpack(acc):
    a_qkv, a_out, a_in, a_back, a_vec = acc
    b_all = a_qkv[D]
    vec = jnp.sum(a_vec, axis=2)
    return (
        a_qkv[0:D],
        jnp.concatenate([b_all[0:D], b_all[2 * D :]]),
        a_out[0:D],
        a_out[D],
        vec[2],
        vec[3],
        a_in[0:D],
        a_in[D],
        a_back[0:FF],
        a_back[FF],
        vec[0],
        vec[1],
    )


def fused(frames, tiles, *args):
    point_feats, point_slot, bucket_len, window_len, w_vfe, b_vfe, gain_vfe = args[:7]
    weights, cotangent = args[7:19], args[19]
    _, pf, points = point_feats.shape
    bucket = points // tiles
    nw = window_len.shape[1]
    n = nw * WSLOT
    any_space = pl.BlockSpec(memory_space=pl.ANY)
    dma = pltpu.SemaphoreType.DMA
    rows = slot_rows(bucket)
    got_feats, got_slots, next_len = pl.pallas_call(
        functools.partial(exchange_kernel, tiles, n),
        out_shape=(
            shape((tiles, pf, bucket), bf16), shape((tiles, rows, D), jnp.int32),
            shape((8, D), jnp.int32),
        ),
        in_specs=[SMEM, SMEM, VMEM, VMEM],
        out_specs=(VMEM, VMEM, VMEM),
        scratch_shapes=[
            pltpu.VMEM((tiles, pf, bucket), bf16), pltpu.VMEM((tiles, rows, D), jnp.int32),
            pltpu.VMEM((8, D), jnp.int32),
            dma((tiles - 1,)), dma((tiles - 1,)), dma((tiles - 1,)), dma((tiles - 1,)),
            dma((1,)), dma((1,)),
        ],
        compiler_params=pltpu.CompilerParams(
            vmem_limit_bytes=VMEM_LIMIT, collective_id=0, has_side_effects=True
        ),
    )(bucket_len, window_len, point_slot, point_feats)
    got_slots = got_slots.reshape(-1)
    b_row = b_vfe[None, :]
    ps, stat = call(
        functools.partial(scatter_kernel, nw),
        (shape((n, D), f32), shape((8, D), f32)),
        2, 5,
        [pltpu.VMEM((bucket, D), f32)] + [pltpu.VMEM((n + 128, D), f32)] * NACC,
        got_slots, window_len, got_feats, w_vfe, b_row,
    )
    spec = main_scratch(frames, tiles, nw, pf, bucket)
    per_f = Reducer.ROWS // frames
    po, gp, full0, full1, small = pl.pallas_call(
        functools.partial(main_kernel, frames, tiles, nw, GROUP, spec),
        out_shape=(
            shape((n, D), bf16), shape((tiles, pf, bucket), bf16), shape((frames, per_f, D), bf16),
            shape((frames, per_f, D), bf16), shape((EXTRA, D), f32),
        ),
        in_specs=[SMEM] * 3 + [any_space] + [VMEM] * 18,
        out_specs=(any_space, any_space, VMEM, VMEM, VMEM),
        scratch_shapes=[entry for entries in spec.values() for entry in entries],
        compiler_params=pltpu.CompilerParams(
            vmem_limit_bytes=MAIN_LIMIT, collective_id=1, has_side_effects=True
        ),
    )(
        got_slots, window_len, next_len, cotangent, stat, ps, got_feats, w_vfe, b_row,
        gain_vfe[None, :], *weights,
    )
    out_shape = (
        shape((1, n, D), bf16), shape((1, pf, points), bf16),
        shape((pf, D), f32), shape((1, D), f32), shape((1, D), f32),
        shape((2, D, 3 * D), f32), shape((2, 2 * D), f32), shape((2, D, D), f32), shape((2, D), f32),
        shape((2, D), f32), shape((2, D), f32), shape((2, D, FF), f32), shape((2, FF), f32),
        shape((2, FF, D), f32), shape((2, D), f32), shape((2, D), f32), shape((2, D), f32),
    )
    outs = pl.pallas_call(
        finish_kernel,
        out_shape=out_shape,
        in_specs=[VMEM] * 5,
        out_specs=(VMEM,) * 17,
        compiler_params=pltpu.CompilerParams(vmem_limit_bytes=VMEM_LIMIT),
    )(po, gp, full0, full1, small)
    return (*outs[:3], outs[3][0], outs[4][0], *outs[5:])


def stepwise(
    tiles, point_feats, point_slot, bucket_len, window_len, w_vfe, b_vfe, gain_vfe, *rest
):
    weights, cotangent = rest[:12], rest[12]
    feats = point_feats[0]
    pf, points = feats.shape
    bucket = points // tiles
    nw = window_len.shape[1]
    n = nw * WSLOT
    half = WSLOT // 2
    live = jnp.arange(bucket, dtype=jnp.int32)[None, :] < bucket_len[0][:, None]
    target = jnp.where(live, point_slot[0].reshape(tiles, bucket), n)
    a2a = functools.partial(lax.all_to_all, axis_name="tile", split_axis=0, concat_axis=0, tiled=True)
    got_feats = a2a(feats.reshape(pf, tiles, bucket).transpose(1, 0, 2))
    target = target[:, : bucket // 2] + target[:, bucket // 2 :] * 65536
    got_slots = a2a(target).reshape(-1)
    lens = jnp.concatenate([window_len[0], passed_along(window_len[0, 0:1], "tile", -1)])
    b_row = b_vfe[None, :]
    acc_rows = n + 128
    ps, stat = call(
        functools.partial(scatter_kernel, nw),
        (shape((n, D), f32), shape((8, D), f32)),
        2, 5,
        [pltpu.VMEM((bucket, D), f32)] + [pltpu.VMEM((acc_rows, D), f32)] * NACC,
        got_slots, window_len, got_feats, w_vfe, b_row,
    )
    sums = lax.psum(stat[0:2], "tile")
    count = sums[1]
    scale = lax.rsqrt(sums[0] / count + EPS)
    coef = (scale * gain_vfe)[None, :]
    fo = call(
        functools.partial(first_forward_kernel, nw, GROUP),
        shape((nw, D, WSLOT), f32), 1, 15, layer_scratch(),
        lens, ps, coef, *weights,
    )
    rim = passed_along(fo[0].astype(bf16), "tile", -1)
    cot = cotangent[0]
    rim_cot = passed_along(cot[:half], "tile", -1)
    acc_out = tuple(shape(a, f32) for a in ACC_SHAPES)
    second = call(
        functools.partial(second_kernel, nw, GROUP),
        (shape((n, D), bf16), shape((nw, D, WSLOT), f32)) + acc_out,
        1, 17,
        layer_scratch() + [pltpu.VMEM((nw + 1, D, WSLOT), f32), pltpu.VMEM((n, D), bf16)],
        lens, fo, rim, cot, rim_cot, *weights,
    )
    view, gv = second[0], second[1]
    back_rim = passed_along(view[n - half :], "tile", 1)
    pillar_out = jnp.concatenate([back_rim, view[: n - half]], axis=0)[None]
    back = passed_along(gv[nw - 1].astype(bf16), "tile", 1)
    first = call(
        functools.partial(first_backward_kernel, nw, GROUP),
        (shape((n, D), f32),) + acc_out,
        1, 17,
        layer_scratch() + [pltpu.VMEM((nw + 1, D, WSLOT), f32)],
        lens, ps, coef, gv, back, *weights,
    )
    d_enc = first[0]
    local_dot = jnp.sum(d_enc * ps, axis=0)
    dots = lax.psum(local_dot, "tile")
    cb = (gain_vfe * scale**3 * dots / count)[None, :]
    out, gw, gb = call(
        functools.partial(gather_kernel, nw),
        (shape((tiles, pf, bucket), bf16), shape((pf, D), f32), shape((8, D), f32)),
        2, 9,
        [pltpu.VMEM((acc_rows, D), f32), pltpu.VMEM((bucket, D), f32)],
        got_slots, window_len, got_feats, w_vfe, b_row, d_enc, ps, coef, cb,
    )
    grad_points = a2a(out).transpose(1, 0, 2).reshape(pf, points)[None]
    g_zero, g_one, g_pts = lax.psum(
        (
            unpack(first[1:]), unpack(second[2:]),
            (gw, jnp.sum(gb, axis=0), local_dot * scale),
        ),
        ("frame", "tile"),
    )
    layer = [jnp.stack([a, b]) for a, b in zip(g_zero, g_one)]
    return (pillar_out, grad_points, *g_pts, *layer)


def local(*args):
    frames, tiles = lax.axis_size("frame"), lax.axis_size("tile")
    bucket = args[0].shape[2] // tiles
    even = Reducer.ROWS % (frames * tiles * 16) == 0 and EXTRA % (tiles * 8) == 0
    if even and bucket % (2 * D) == 0:
        return fused(frames, tiles, *args)
    return stepwise(tiles, *args)


def solution(mesh):
    rep = P()
    rows = P("frame", "tile")
    return jax.shard_map(
        local,
        mesh=mesh,
        in_specs=(P("frame", None, "tile"), rows, rows, rows)
        + (rep,) * 15
        + (P("frame", "tile", None),),
        out_specs=(P("frame", "tile", None), P("frame", None, "tile")) + (rep,) * 15,
        check_vma=False,
    )
```

time: 1090 us -> 146 us (0.13); the launches traced: 1080 us -> 146 us
  matrix products: 279 us -> 0 us
  waiting for transfers between devices: 257 us -> 0 us
  local copies, waits for them, and re-layouts: 235 us -> 0 us
  other arithmetic: 200 us -> 0 us
  Pallas kernels: 0 us -> 145 us
  blocking collectives: 68 us -> 0 us
  starting transfers between devices: 22.2 us -> 0 us
  between operations: 15.6 us -> 0.83 us
    dot_general x167 -> x0, matrix products: 279 us -> none  [the longest x40 72 us: block_scores(): jnp.einsum('wqhd,wkhd->whqk', query_blk, key_blk, preferred_element_type=...]
    psum x1 -> x0, waiting for transfers between devices: 149 us -> none  [local(): lax.psum((grad_w_vfe, grad_b_vfe, grad_gain_local, grads_zero[0], grads_z...]
    pallas_call x0 -> x4, Pallas kernels: none -> 145 us  [the longest x1 105 us: fused(): pl.pallas_call(functools.partial(main_kernel, frames, tiles, nw, GROUP, s...]
    ppermute x5 -> x0, waiting for transfers between devices: 77.9 us -> none  [passed_along(): return lax.ppermute(value, axis, pairs)]
    psum x3 -> x0, blocking collectives: 68 us -> none  [the longest x1 39.5 us: local(): lax.psum((grad_w_vfe, grad_b_vfe, grad_gain_local, grads_zero[0], grads_z...]
    scatter-add x1 -> x0, other arithmetic: 67.8 us -> none  [segment_rows(): jax.ops.segment_sum(hidden_rows, targets, num_segments=slot_count + 1)]
    reduce_sum x41 -> x0, other arithmetic: 66.8 us -> none  [the longest x4 17.7 us: layer_norm(): center = values - jnp.mean(values, axis=-1, keepdims=True)]
    reshape x16 -> x0, local copies, waits for them, and re-layouts: 54.5 us -> none  [the longest x8 27.5 us: split_blocks(): values.reshape(row_count // (ATT_WIN * WSLOT), ATT_WIN, WSLOT, HEADS, mod...]
  transfers between devices with their start and end apart: 9 -> 0, of which waited for: 5 -> 0; matrix products, arithmetic and copies ran while one was open for 47% -> 0% of each run, Pallas kernels for 0% -> 0%
where the time goes in v1:
time: 146 us
  Pallas kernels  145 us (99%)
    pallas_call x1, Pallas kernels, fused(): pl.pallas_call(functools.partial(main_kernel, frames, tiles, nw, GROUP, s...  105 us
    pallas_call x1, Pallas kernels, call(): pl.pallas_call(kernel, out_shape=out_shape, in_specs=[SMEM] * n_smem + [V...  21.2 us
    pallas_call x1, Pallas kernels, fused(): pl.pallas_call(functools.partial(exchange_kernel, tiles, n), out_shape=(s...  16.1 us
    pallas_call x1, Pallas kernels, fused(): pl.pallas_call(finish_kernel, out_shape=out_shape, in_specs=[VMEM] * 5, o...  3.18 us

profile of v1, /device:TPU:0, one launch (start us, length us, event | category | flops | bytes accessed | tf_op | source)
XLA Modules:
  0.0 146.0 jit_solution(4221971413199587791)
XLA Ops:
  0.7 16.1 %shard_map.323 = (bf16[8,16,1280]{2,1,0:T(8,128)(2,1)}, s32[8,8,128]{2,1,0:T(8,128)}, s32[8,128]{1,0:T(8,128)}) custom-call(s32[1,8]{1,0:T(1,128)} %blen.1, s32[1,40]{1,0:T(1,128)} %refs_1_.1, s32[1,10240]{1,0:T(1,128)} %slot.1, bf16[1,16,10240]{2,1,0:T(8,128)(2,1)} %feats.1), custom_call_target="tpu_custom_call" | custom-call | tf_op jit(solution)/shard_map/pallas_call | solution.py:1259
  16.8 21.2 %shard_map.324 = (f32[5120,128]{1,0:T(8,128)}, f32[8,128]{1,0:T(8,128)}) custom-call(s32[8192]{0:T(1024)} %bitcast.5, s32[1,40]{1,0:T(1,128)} %refs_1_.1, bf16[8,16,1280]{2,1,0:T(8,128)(2,1)} %get-tuple-element.46.feats.refs_6_, bf16[16,128]{1,0:T(8,128)(2,1)} %refs_7_.1, f32[1,128]{1,0:T(1,128)} %bitcast.7), custom_call_target="tpu_custom_call" | custom-call | tf_op jit(solution)/shard_map/pallas_call | solution.py:1214
  38.0 104.7 %shard_map.325 = (bf16[5120,128]{1,0:T(8,128)(2,1)}, bf16[8,16,1280]{2,1,0:T(8,128)(2,1)}, bf16[4,256,128]{2,1,0:T(8,128)(2,1)}, bf16[4,256,128]{2,1,0:T(8,128)(2,1)}, f32[64,128]{1,0:T(8,128)}) custom-call(s32[8192]{0:T(1024)} %bitcast.6, s32[1,40]{1,0:T(1,128)} %refs_1_.1, s32[8,128]{1,0:T(8,128)} %get-tuple-element.45.refs_2_, ...), custom_call_target="tpu_custom_call" | custom-call | tf_op jit(solution)/shard_map/pallas_call | solution.py:1288
  142.6 3.2 %shard_map.326 = (bf16[1,5120,128]{2,1,0:T(8,128)(2,1)}, bf16[1,16,10240]{2,1,0:T(8,128)(2,1)}, f32[16,128]{1,0:T(8,128)}, f32[1,128]{1,0:T(1,128)}, f32[1,128]{...) custom-call(bf16[5120,128]{1,0:T(8,128)(2,1)} %get-tuple-element.49., ...), custom_call_target="tpu_custom_call" | custom-call | tf_op jit(solution)/shard_map/pallas_call | solution.py:1311
